TPU v7x, 32 devices: a whole 2x2x4 slice. The times are simulated.
32 devices in a mesh: clips: 2 (over x), patch: 16 (over z, y, core).
Axes of the slice: x: 2, y: 2, z: 4, core: 2. Of those that a mesh axis runs over, the one named last changes fastest.
Arguments:
- q_video: bfloat16 [2304, 1536], P(('clips', 'patch')), parts along dimension 0, may hold values from -6 to 6
- k_video: bfloat16 [2304, 1536], P(('clips', 'patch')), parts along dimension 0, may hold values from -6 to 6
- v_video: bfloat16 [2304, 1536], P(('clips', 'patch')), parts along dimension 0, may hold values from -6 to 6
- k_stale: bfloat16 [2304, 1536], P(('clips', 'patch')), parts along dimension 0, may hold values from -6 to 6
- v_stale: bfloat16 [2304, 1536], P(('clips', 'patch')), parts along dimension 0, may hold values from -6 to 6
- q_text: bfloat16 [128, 1536], P(('clips', 'patch')), parts along dimension 0, may hold values from -6 to 6
- k_text: bfloat16 [128, 1536], P(('clips', 'patch')), parts along dimension 0, may hold values from -6 to 6
- v_text: bfloat16 [128, 1536], P(('clips', 'patch')), parts along dimension 0, may hold values from -6 to 6
- q_gain: float32 [128], replicated, may hold values from 0.6 to 4
- k_gain: float32 [128], replicated, may hold values from 0.6 to 4
- out_weight: bfloat16 [1536, 3072], replicated, may hold values from -0.15625 to 0.15625
Outputs:
- video_out: bfloat16 [2304, 3072], P(('clips', 'patch')), parts along dimension 0
- text_out: bfloat16 [128, 3072], P(('clips', 'patch')), parts along dimension 0
There are 2 independent parts, one for each index of `clips`. A program takes and returns all parts, laid end to end along the dimension named above; an argument that names none is the same for every part. Nothing has to cross between parts.
All inputs are finite; a program needn't handle non-finite values.
Results may differ from a plain program's by a relative error of at most 0.012.
The roundings to bfloat16 on the way count: a program that leaves them out, or rounds other values in their place, can miss the bound.
Values may be sent and summed in bfloat16 or wider, within the bound.
A program may use at most 128 MiB of HBM per device.

v0:
```python
import jax
import jax.numpy as jnp
from jax import lax
from jax.sharding import PartitionSpec as P


def normed(rows, gain):
    heads = rows.astype(jnp.float32).reshape(rows.shape[0], -1, gain.shape[0])
    scaled = heads * lax.rsqrt(jnp.mean(heads * heads, axis=-1, keepdims=True) + 1e-06) * gain
    return scaled.reshape(rows.shape[0], -1).astype(jnp.bfloat16)


def scores(queries, keys, head_size):
    keyed = keys.reshape(keys.shape[0], -1, head_size)
    raw = jnp.einsum("rhd,phd->hrp", queries, keyed, preferred_element_type=jnp.float32)
    return raw / jnp.sqrt(jnp.float32(head_size))


def update(carry, score, values, head_size):
    top, total, summed = carry
    top_new = jnp.maximum(top, jnp.max(score, axis=-1))
    factor = jnp.exp(top - top_new)
    expo = jnp.exp(score - top_new[:, :, None])
    total = total * factor + jnp.sum(expo, axis=-1)
    valued = values.reshape(values.shape[0], -1, head_size)
    added = jnp.einsum(
        "hrp,phd->rhd", expo.astype(jnp.bfloat16), valued, preferred_element_type=jnp.float32
    )
    summed = summed * jnp.transpose(factor)[:, :, None] + added
    return (top_new, total, summed)


def body(
    q_video, k_video, v_video, k_stale, v_stale, q_text, k_text, v_text, q_gain, k_gain, out_weight
):
    head_size = q_gain.shape[0]
    tok_rows = q_video.shape[0]
    width = q_video.shape[1]
    head_count = width // head_size
    queries = jnp.concatenate([normed(q_video, q_gain), normed(q_text, q_gain)], axis=0)
    queries = queries.reshape(-1, head_count, head_size)
    fresh_keys = normed(k_video, k_gain)
    stale_keys = normed(k_stale, k_gain)
    text_keys = normed(k_text, k_gain)
    mine = lax.axis_index("patch")
    query_rows = queries.shape[0]
    all_text_keys, all_text_values = (
        lax.all_gather(text_keys, "patch", axis=0, tiled=True),
        lax.all_gather(v_text, "patch", axis=0, tiled=True),
    )
    first = scores(queries, jnp.concatenate([fresh_keys, all_text_keys], axis=0), head_size)
    top = jnp.max(first, axis=-1)
    empty = (top, jnp.zeros_like(top), jnp.zeros((query_rows, head_count, head_size), jnp.float32))
    carry = update(empty, first, jnp.concatenate([v_video, all_text_values], axis=0), head_size)
    pieces = (
        lax.all_gather(stale_keys, "patch", axis=0, tiled=True),
        lax.all_gather(v_stale, "patch", axis=0, tiled=True),
    )
    ident = jnp.arange(pieces[0].shape[0], dtype=jnp.int32)
    masked = ident // tok_rows == mine
    score = scores(queries, pieces[0], head_size)
    score = jnp.where(masked[None, None, :], -jnp.inf, score)
    carry = update(carry, score, pieces[1], head_size)
    top, total, summed = carry
    attended = (
        (summed / jnp.transpose(total)[:, :, None]).reshape(query_rows, width).astype(jnp.bfloat16)
    )
    projected = jnp.dot(attended, out_weight, preferred_element_type=jnp.float32).astype(
        jnp.bfloat16
    )
    return (projected[:tok_rows], projected[tok_rows:])


def solution(mesh):
    placed = (
        P(("clips", "patch"), None),
        P(("clips", "patch"), None),
        P(("clips", "patch"), None),
        P(("clips", "patch"), None),
        P(("clips", "patch"), None),
        P(("clips", "patch"), None),
        P(("clips", "patch"), None),
        P(("clips", "patch"), None),
        P(),
        P(),
        P(),
    )
    return jax.shard_map(
        body,
        mesh=mesh,
        in_specs=placed,
        out_specs=(P(("clips", "patch"), None), P(("clips", "patch"), None)),
        check_vma=False,
    )
```

profile of v0, /device:TPU:1, one launch (start us, length us, event | category | flops | bytes accessed | tf_op | source)
XLA Modules:
  0.0 133.8 jit_solution(14254674676857655945)
XLA Ops:
  7.2 0.0 copy-start
  7.2 0.0 copy-start.4
  7.2 0.0 copy-start.3
  7.2 0.0 copy-start.5
  7.2 0.0 all-gather.5.cloned.1.call-start
  7.3 0.6 copy-done
  7.8 1.0 convert_multiply_fusion.3
  8.8 0.1 mul.170
  8.9 0.2 reduce_sum.69
  9.1 0.0 copy-start.13
  9.1 0.0 copy-start.12
  9.2 1.0 convert_multiply_fusion.1
  10.1 0.0 copy-start.15
  10.2 0.1 mul.187
  10.2 0.0 copy-start.16
  10.3 0.2 reduce_sum.71
  10.5 0.2 mul.171
  10.7 0.2 mul.188
  10.9 0.0 copy-done.4
  10.9 0.0 copy-done.3
  11.0 1.0 fusion.27
  12.0 0.0 all-gather.5.cloned.1.call-update
  12.0 0.0 all-gather.7.cloned.1.call-start
  12.1 0.7 all-gather.7.cloned.1.call-update
  12.8 0.0 copy-done.5
  12.8 0.1 mul.154
  12.9 0.2 reduce_sum.67
  13.2 0.1 reduce_sum.68
  13.3 0.1 reduce_sum.70
  13.4 0.1 broadcast_bitcast_fusion
  13.5 23.9 %all-gather = bf16[16,4,1536]{2,1,0:T(4,128)(2,1)S(1)} all-gather(bf16[1,4,1536]{2,1,0:T(4,128)(2,1)S(1)} %fusion.39), channel_id=1, replica_groups=mesh['clips'=2,'patch'=16] {'patch'}, dimensions={0}, use_global_device_ids=true | all-gather | bytes 208896 | tf_op jit(solution)/shard_map/all_gather | solution.py:48
  37.4 0.1 reshape.116
  37.5 18.3 %all-gather.1 = bf16[16,4,1536]{2,1,0:T(4,128)(2,1)S(1)} all-gather(bf16[1,4,1536]{2,1,0:T(4,128)(2,1)S(1)} %bitcast.105), channel_id=1, replica_groups=mesh['clips'=2,'patch'=16] {'patch'}, dimensions={0}, use_global_device_ids=true | all-gather | bytes 208896 | tf_op jit(solution)/shard_map/all_gather | solution.py:49
  55.8 0.7 reshape.118
  56.6 0.1 broadcast_bitcast_fusion.1
  56.7 0.0 copy-start.11
  56.7 0.2 mul.155
  56.9 0.2 copy_bitcast_fusion
  57.1 0.0 copy-start.2
  57.1 0.7 copy-done.2
  57.8 0.4 fusion.52
  58.2 1.0 copy-done.6
  59.2 0.7 fusion.20
  59.9 2.5 %all-gather.5.cloned.1.call-done = bf16[1152,1536]{1,0:T(8,128)(2,1)} async-done(((bf16[72,1536]{1,0:T(8,128)(2,1)}), bf16[1152,1536]{1,0:T(8,128)(2,1)}) %all-gather.5.cloned.1.call-update) | async-done | bytes 3538960 | tf_op jit(solution)/shard_map/all_gather | solution.py:56
  62.5 4.4 %copy.24 = bf16[1152,1536]{0,1:T(8,128)(2,1)S(1)} copy(bf16[1152,1536]{1,0:T(8,128)(2,1)} %all-gather.5.cloned.1.call-done) | data formatting | bytes 7077888 | tf_op jit(solution)/shard_map/all_gather | solution.py:56
  66.9 0.0 copy-start.17
  66.9 2.0 %fusion.53 = (f32[12,76]{1,0:T(8,128)S(1)}, f32[12,76,1152]{2,1,0:T(8,128)S(1)}) fusion(bf16[1152,12,128]{0,2,1:T(8,128)(2,1)S(1)} %bitcast.98, bf16[4,12,128]{2,0,1:T(4,128)(2,1)} %copy-done.11, bf16[72,12,128]{2,0,1:T(8,128)(2,1)} %copy-done.2, pred[1152]{0:T(1024)(128)(4,1)S(1)} %fusion.41), kind=kOutput, calls=%fused_computation.79 | convolution fusion | flops 272577664 | bytes 7979712 | tf_op jit(solution)/shard_map/rhd,phd->hrp/dot_general | solution.py:15
  68.9 0.0 copy-start.9
  68.9 2.0 %copy-done.1 = f32[12,76,1152]{2,1,0:T(8,128)} copy-done((f32[12,76,1152]{2,1,0:T(8,128)}, f32[12,76,1152]{2,1,0:T(8,128)S(1)}, u32[]{:S(2)}) %copy-start.1) | copy-done | bytes 4202520
  70.9 0.9 fusion.1
  71.8 0.0 copy-done.14
  71.8 0.6 bitcast_add_fusion
  72.4 0.0 copy-done.9
  72.4 0.0 copy-done.8
  72.4 1.4 %fusion.13 = f32[76,12,128]{2,0,1:T(8,128)} fusion(f32[12,76,136]{1,2,0:T(8,128)S(1)} %copy-done.7, f32[12,76]{1,0:T(8,128)S(1)} %get-tuple-element.7, f32[76,12]{0,1:T(8,128)S(1)} %get-tuple-element.3, f32[76,12]{0,1:T(8,128)S(1)} %get-tuple-element.4, bf16[64,1536]{1,0:T(8,128)(2,1)S(1)} %copy-done.8, bf16[72,1536]{1,0:T(8,128)(2,1)S(1)} %copy-done.17), kind=kOutput, calls=%fused_computation.13 | convolution fusion | flops 33069312 | bytes 1391808 | tf_op jit(solution)/shard_map/hrp,phd->rhd/dot_general | solution.py:26
  73.8 37.7 %all-gather.7.cloned.1.call-done = bf16[1152,1536]{1,0:T(8,128)(2,1)} async-done(((bf16[72,1536]{1,0:T(8,128)(2,1)}), bf16[1152,1536]{1,0:T(8,128)(2,1)}) %all-gather.7.cloned.1.call-update) | async-done | bytes 3538960 | tf_op jit(solution)/shard_map/all_gather | solution.py:57
  111.5 4.4 %copy.26 = bf16[1152,1536]{0,1:T(8,128)(2,1)S(1)} copy(bf16[1152,1536]{1,0:T(8,128)(2,1)} %all-gather.7.cloned.1.call-done) | data formatting | bytes 7077888 | tf_op jit(solution)/shard_map/all_gather | solution.py:57
  115.9 4.1 %fusion.17 = bf16[76,12,128]{2,0,1:T(8,128)(2,1)S(1)} fusion(f32[76,12,128]{2,0,1:T(8,128)} %fusion.13, bf16[1152,12,128]{0,2,1:T(8,128)(2,1)S(1)} %bitcast.99, f32[12,76,1152]{2,1,0:T(8,128)} %copy-done.1, f32[12,76]{1,0:T(8,128)S(1)} %copy-done.10, f32[76,12]{0,1:T(8,128)} %get-tuple-element.2), kind=kOutput, calls=%fused_computation.15 | convolution fusion | flops 271411200 | bytes 8449152 | tf_op jit(solution)/shard_map/hrp,phd->rhd/dot_general | solution.py:26
  119.9 0.1 copy.28
  120.0 0.1 pad.6
  120.1 0.1 copy.39
  120.2 5.4 %convolution_convert_fusion = bf16[76,3072]{1,0:T(8,128)(2,1)S(1)} fusion(bf16[76,1536]{1,0:T(8,128)(2,1)S(1)} %bitcast.103, bf16[1536,3072]{1,0:T(8,128)(2,1)} %param.21), kind=kOutput, calls=%fused_computation.5 | convolution fusion | flops 717459456 | bytes 10137600 | tf_op jit(solution)/shard_map/dot_general | solution.py:68
  125.6 0.8 slice.8
  126.4 0.6 slice.9
  (30 shorter events, 0.2 us)
Async XLA Ops:
  7.2 0.7 copy-start
  7.2 3.8 %copy-start.4 = (bf16[72,1536]{1,0:T(8,128)(2,1)S(1)}, bf16[72,1536]{1,0:T(8,128)(2,1)}, u32[]{:S(2)}) copy-start(bf16[72,1536]{1,0:T(8,128)(2,1)} %param.12) | copy-start | bytes 663556
  7.2 3.8 %copy-start.3 = (bf16[72,1536]{1,0:T(8,128)(2,1)S(1)}, bf16[72,1536]{1,0:T(8,128)(2,1)}, u32[]{:S(2)}) copy-start(bf16[72,1536]{1,0:T(8,128)(2,1)} %param.14) | copy-start | bytes 663556
  7.2 5.6 %copy-start.5 = (bf16[72,1536]{1,0:T(8,128)(2,1)S(1)}, bf16[72,1536]{1,0:T(8,128)(2,1)}, u32[]{:S(2)}) copy-start(bf16[72,1536]{1,0:T(8,128)(2,1)} %param.11) | copy-start | bytes 663556
  7.2 55.3 %all-gather.5.cloned.1.call-start = ((), (), s32[]{:S(2)}) async-start(), calls=%async_computation | async-start | bytes 3760128 | tf_op jit(solution)/shard_map/all_gather | solution.py:56
  9.1 4.0 %copy-start.13 = (bf16[4,1536]{1,0:T(4,128)(2,1)S(1)}, bf16[4,1536]{1,0:T(4,128)(2,1)}, u32[]{:S(2)}) copy-start(bf16[4,1536]{1,0:T(4,128)(2,1)} %param.16) | copy-start | bytes 36868
  9.1 4.1 %copy-start.12 = (bf16[4,1536]{1,0:T(4,128)(2,1)S(1)}, bf16[4,1536]{1,0:T(4,128)(2,1)}, u32[]{:S(2)}) copy-start(bf16[4,1536]{1,0:T(4,128)(2,1)} %param.17) | copy-start | bytes 36868
  10.1 27.3 %copy-start.15 = (bf16[4,1536]{1,0:T(4,128)(2,1)S(1)}, bf16[4,1536]{1,0:T(4,128)(2,1)}, u32[]{:S(2)}) copy-start(bf16[4,1536]{1,0:T(4,128)(2,1)} %param.18) | copy-start | bytes 36868
  10.2 46.3 %copy-start.16 = (f32[128]{0:T(128)S(1)}, f32[128]{0:T(128)}, u32[]{:S(2)}) copy-start(f32[128]{0:T(128)} %param.19) | copy-start | bytes 1540
  12.0 99.5 %all-gather.7.cloned.1.call-start = ((), (), s32[]{:S(2)}) async-start(), calls=%async_computation.1 | async-start | bytes 3760128 | tf_op jit(solution)/shard_map/all_gather | solution.py:57
  56.7 3.2 %copy-start.11 = (bf16[4,12,128]{2,0,1:T(4,128)(2,1)}, bf16[4,12,128]{2,0,1:T(4,128)(2,1)S(1)}, u32[]{:S(2)}) copy-start(bf16[4,12,128]{2,0,1:T(4,128)(2,1)S(1)} %fusion.40) | copy-start | bytes 36868
  57.1 0.7 copy-start.2
  58.2 1.0 copy-start.6
  66.8 4.9 %copy-start.14 = (f32[12,76]{1,0:T(8,128)S(1)}, f32[12,76]{1,0:T(8,128)}, u32[]{:S(2)}) copy-start(f32[12,76]{1,0:T(8,128)} %fusion.20) | copy-start | bytes 10948
  66.9 5.5 %copy-start.7 = (f32[12,76,136]{1,2,0:T(8,128)S(1)}, f32[12,76,136]{1,2,0:T(8,128)}, u32[]{:S(2)}) copy-start(f32[12,76,136]{1,2,0:T(8,128)} %copy-done.6) | copy-start | bytes 1488388
  66.9 5.5 %copy-start.8 = (bf16[64,1536]{1,0:T(8,128)(2,1)S(1)}, bf16[64,1536]{1,0:T(8,128)(2,1)}, u32[]{:S(2)}) copy-start(bf16[64,1536]{1,0:T(8,128)(2,1)} %reshape.118) | copy-start | bytes 589828
  66.9 5.5 %copy-start.17 = (bf16[72,1536]{1,0:T(8,128)(2,1)S(1)}, bf16[72,1536]{1,0:T(8,128)(2,1)}, u32[]{:S(2)}) copy-start(bf16[72,1536]{1,0:T(8,128)(2,1)} %param.13) | copy-start | bytes 663556
  68.9 2.0 %copy-start.1 = (f32[12,76,1152]{2,1,0:T(8,128)}, f32[12,76,1152]{2,1,0:T(8,128)S(1)}, u32[]{:S(2)}) copy-start(f32[12,76,1152]{2,1,0:T(8,128)S(1)} %get-tuple-element.10) | copy-start | bytes 12607492
  68.9 3.5 %copy-start.9 = (f32[12,76]{1,0:T(8,128)}, f32[12,76]{1,0:T(8,128)S(1)}, u32[]{:S(2)}) copy-start(f32[12,76]{1,0:T(8,128)S(1)} %max.13) | copy-start | bytes 10948
  73.8 42.1 %copy-start.10 = (f32[12,76]{1,0:T(8,128)S(1)}, f32[12,76]{1,0:T(8,128)}, u32[]{:S(2)}) copy-start(f32[12,76]{1,0:T(8,128)} %copy-done.9) | copy-start | bytes 10948
Sparse Core Ops, SparseCore 0:
  12.1 50.2 all-gather.4
  64.8 46.7 all-gather.6
where the time goes:
time: 134 us
  blocking collectives  42.2 us (31%)
  waiting for transfers between devices  40.9 us (31%)
  local copies, waits for them, and re-layouts  16.5 us (12%)
  between operations  14.5 us (11%)
  matrix products  13.2 us (10%)
  other arithmetic  6.39 us (5%)
    all_gather x1, waiting for transfers between devices, body(): lax.all_gather(v_stale, 'patch', axis=0, tiled=True)  37.7 us
    all_gather x1, blocking collectives, body(): lax.all_gather(text_keys, 'patch', axis=0, tiled=True)  23.9 us
    all_gather x1, blocking collectives, body(): lax.all_gather(v_text, 'patch', axis=0, tiled=True)  18.3 us
    dot_general x2, matrix products, update(): jnp.einsum('hrp,phd->rhd', expo.astype(jnp.bfloat16), valued, preferred_e...  5.45 us
    dot_general x1, matrix products, body(): jnp.dot(attended, out_weight, preferred_element_type=jnp.float32)  5.43 us
    unnamed x42, local copies, waits for them, and re-layouts  5.38 us
    all_gather x1, local copies, waits for them, and re-layouts, body(): lax.all_gather(stale_keys, 'patch', axis=0, tiled=True)  4.36 us
    all_gather x1, local copies, waits for them, and re-layouts, body(): lax.all_gather(v_stale, 'patch', axis=0, tiled=True)  4.36 us
  transfers between devices with their start and end apart: 2, of which 2 were waited for; matrix products, arithmetic and copies ran while one was open for 9% of the time, Pallas kernels for 0%

commit v1 on v0

v1 whole, which is shorter than its diff:
```python
import functools
import math

import jax
import jax.numpy as jnp
from jax import lax
from jax.experimental import pallas as pl
from jax.experimental.pallas import tpu as pltpu
from jax.sharding import PartitionSpec as P

QUAD = 4
LOW = -1e30
KEY, VALUE, QUERY, FRESH_KEY, FRESH_VALUE = range(5)


def kernel(
    n, tok, txt, size,
    q_video, k_video, v_video, k_stale, v_stale, q_text, k_text, v_text, q_gain, k_gain, w_hbm,
    video_out, text_out,
    rows_f32, outgoing, kv, quad, bias, queries, keybuf, score, acc, total, att_out, att_in, weight,
    send_sem, recv_sem, fwd_send, quad_send, quad_recv, att_send, att_recv, w_sem,
):
    f32, bf16 = jnp.float32, jnp.bfloat16
    pad = outgoing.shape[2]
    part = outgoing.shape[3]
    heads = part // size
    wide = QUAD * pad
    column = n // 2
    quads = column // QUAD
    nblocks = 2 * quads + 1

    me = lax.axis_index("patch")
    plane, side, core = me // 4, (me // 2) % 2, me % 2
    spot = plane * 2 + core
    zz, mine = spot // QUAD, spot % QUAD

    def device(place, at_side):
        return {"patch": ((place // 2) * 2 + at_side) * 2 + place % 2}

    across = device(spot, 1 - side)

    barrier = pltpu.get_barrier_semaphore()

    def greet(d, _):
        pl.semaphore_signal(barrier, inc=1, device_id=device((spot + d) % column, side))
        return 0

    lax.fori_loop(1, column, greet, 0)
    pl.semaphore_signal(barrier, inc=1, device_id=across)
    w_copy = pltpu.make_async_copy(w_hbm, weight, w_sem)
    w_copy.start()
    rows_f32[tok:, :] = jnp.zeros((pad - tok, rows_f32.shape[1]), f32)

    def prepare(kind, video, text, gain):
        if text is not None:
            rows_f32[tok : tok + txt, :] = text[...].astype(f32)
        rows_f32[:tok, :] = video[...].astype(f32)
        for h in range(QUAD * heads):
            x = rows_f32[:, h * size : (h + 1) * size]
            if gain is not None:
                x = x * lax.rsqrt(jnp.mean(x * x, axis=-1, keepdims=True) + 1e-06) * gain[...]
            lane = (h % heads) * size
            outgoing[kind, h // heads, :, lane : lane + size] = x.astype(bf16)

    def distance(i):
        return 1 + (i + column // 2 - 1) % (column - 1)

    def column_copy(kind, i):
        to = (spot + distance(i)) % column
        return pltpu.make_async_remote_copy(
            src_ref=outgoing.at[kind, to % QUAD],
            dst_ref=kv.at[kind, 0, zz, mine],
            send_sem=send_sem.at[kind, i],
            recv_sem=recv_sem.at[kind, 0, spot],
            device_id=device(to, side),
        )

    def column_arrival(kind, from_side, place):
        slot = kv.at[kind, from_side, place // QUAD, place % QUAD]
        return pltpu.make_async_remote_copy(
            src_ref=slot,
            dst_ref=slot,
            send_sem=fwd_send.at[kind, place],
            recv_sem=recv_sem.at[kind, from_side, place],
            device_id=across,
        )

    def forward(kind, place):
        return pltpu.make_async_remote_copy(
            src_ref=kv.at[kind, 0, place // QUAD, place % QUAD],
            dst_ref=kv.at[kind, 1, place // QUAD, place % QUAD],
            send_sem=fwd_send.at[kind, place],
            recv_sem=recv_sem.at[kind, 1, place],
            device_id=across,
        )

    def send_column(kind):
        def go(i, _):
            column_copy(kind, i).start()
            return 0

        kv[kind, 0, zz, mine] = outgoing[kind, mine]
        forward(kind, spot).start()
        lax.fori_loop(0, column - 1, go, 0)

    def quad_copy(kind, e):
        to = (mine + e) % QUAD
        return pltpu.make_async_remote_copy(
            src_ref=outgoing.at[kind, to],
            dst_ref=quad.at[kind - QUERY, mine],
            send_sem=quad_send.at[kind - QUERY, e],
            recv_sem=quad_recv.at[kind - QUERY, mine],
            device_id=device(zz * QUAD + to, side),
        )

    def quad_arrival(kind, e):
        slot = quad.at[kind - QUERY, (mine + e) % QUAD]
        return pltpu.make_async_remote_copy(
            src_ref=slot,
            dst_ref=slot,
            send_sem=quad_send.at[kind - QUERY, e],
            recv_sem=quad_recv.at[kind - QUERY, (mine + e) % QUAD],
            device_id=across,
        )

    def send_quad(kind):
        quad[kind - QUERY, mine] = outgoing[kind, mine]
        for e in range(1, QUAD):
            quad_copy(kind, e).start()

    def wait_and_forward(kind):
        def go(i, _):
            place = (spot + column - distance(i)) % column
            column_arrival(kind, 0, place).wait_recv()
            forward(kind, place).start()
            return 0

        lax.fori_loop(0, column - 1, go, 0)

    prepare(KEY, k_stale, k_text, k_gain)
    pl.semaphore_wait(barrier, column)
    send_column(KEY)
    prepare(QUERY, q_video, q_text, q_gain)
    send_quad(QUERY)
    prepare(FRESH_KEY, k_video, None, k_gain)
    send_quad(FRESH_KEY)
    prepare(VALUE, v_stale, v_text, None)
    send_column(VALUE)
    prepare(FRESH_VALUE, v_video, None, None)
    send_quad(FRESH_VALUE)

    def group(index):
        return sum((index >= pad * g).astype(jnp.int32) for g in range(1, QUAD))

    row = lax.broadcasted_iota(jnp.int32, (wide, wide), 0)
    col = lax.broadcasted_iota(jnp.int32, (wide, wide), 1)
    col_group = group(col)
    same = group(row) == col_group
    inner = col - col_group * pad
    bias[0] = jnp.where(inner >= tok + txt, LOW, 0.0)
    bias[1] = jnp.where((inner >= tok + txt) | (same & (inner < tok)), LOW, 0.0)
    bias[2] = jnp.where(same & (inner < tok), 0.0, LOW)

    wait_and_forward(KEY)
    for kind in (QUERY, FRESH_KEY):
        for e in range(1, QUAD):
            quad_arrival(kind, e).wait_recv()

    for h in range(heads):
        queries[h] = quad[0, :, :, h * size : (h + 1) * size].reshape(wide, size)

    def score_block(b, keys, which):
        for h in range(heads):
            keybuf[h] = keys(h * size)
        for h in range(heads):
            lane = h * size
            s = lax.dot_general(queries[h], keybuf[h], (((1,), (1,)), ((), ())), preferred_element_type=f32)
            score[b, h] = s + bias[which]

    def gathered(kind, from_side, z):
        return lambda lane: kv[kind, from_side, z, :, :, lane : lane + size].reshape(wide, size)

    def exchanged(kind):
        return lambda lane: quad[kind - QUERY, :, :, lane : lane + size].reshape(wide, size)

    score_block(0, exchanged(FRESH_KEY), 2)
    score_block(1, gathered(KEY, 0, zz), 1)

    def own_side(e, _):
        score_block(1 + e, gathered(KEY, 0, (zz + e) % quads), 0)
        return 0

    lax.fori_loop(1, quads, own_side, 0)
    wait_and_forward(VALUE)

    def other_side(e, _):
        z = (zz + e) % quads
        for g in range(QUAD):
            column_arrival(KEY, 1, z * QUAD + g).wait_recv()
        score_block(1 + quads + e, gathered(KEY, 1, z), 0)
        return 0

    lax.fori_loop(0, quads, other_side, 0)

    chunk = 64
    factor = math.log2(math.e) / math.sqrt(size)

    def softmax(i, _):
        h, r = i // (wide // chunk), i % (wide // chunk)
        rows = pl.ds(pl.multiple_of(r * chunk, chunk), chunk)
        top = score[0, h, rows, :]
        for b in range(1, nblocks):
            top = jnp.maximum(top, score[b, h, rows, :])
        top = jnp.max(top, axis=-1, keepdims=True)
        added = jnp.zeros((chunk, wide), f32)
        for b in range(nblocks):
            e = jnp.exp2((score[b, h, rows, :] - top) * factor)
            added = added + e
            score[b, h, rows, :] = e
        total[h, rows, :] = jnp.broadcast_to(jnp.sum(added, axis=-1, keepdims=True), (chunk, size))
        return 0

    lax.fori_loop(0, heads * (wide // chunk), softmax, 0)

    def value_block(b, values, first=False):
        for h in range(heads):
            lane = h * size
            o = jnp.dot(score[b, h].astype(bf16), values(lane), preferred_element_type=f32)
            acc[h] = o if first else acc[h] + o

    for e in range(1, QUAD):
        quad_arrival(FRESH_VALUE, e).wait_recv()
    value_block(0, exchanged(FRESH_VALUE), True)

    def own_values(e, _):
        value_block(1 + e, gathered(VALUE, 0, (zz + e) % quads))
        return 0

    lax.fori_loop(0, quads, own_values, 0)

    def other_values(e, _):
        z = (zz + e) % quads
        for g in range(QUAD):
            column_arrival(VALUE, 1, z * QUAD + g).wait_recv()
        value_block(1 + quads + e, gathered(VALUE, 1, z))
        return 0

    lax.fori_loop(0, quads, other_values, 0)

    for h in range(heads):
        done = (acc[h] / total[h]).astype(bf16)
        att_out[:, :, h * size : (h + 1) * size] = done.reshape(QUAD, pad, size)

    def att_copy(e):
        to = (mine + e) % QUAD
        return pltpu.make_async_remote_copy(
            src_ref=att_out.at[to],
            dst_ref=att_in.at[mine],
            send_sem=att_send.at[e],
            recv_sem=att_recv.at[mine],
            device_id=device(zz * QUAD + to, side),
        )

    def att_arrival(e):
        slot = att_in.at[(mine + e) % QUAD]
        return pltpu.make_async_remote_copy(
            src_ref=slot,
            dst_ref=slot,
            send_sem=att_send.at[e],
            recv_sem=att_recv.at[(mine + e) % QUAD],
            device_id=across,
        )

    for e in range(1, QUAD):
        att_copy(e).start()
    att_in[mine] = att_out[mine]
    w_copy.wait()
    for e in range(1, QUAD):
        att_arrival(e).wait_recv()

    step = 512
    attended = jnp.concatenate([att_in[g] for g in range(QUAD)], axis=1)

    def project(i, _):
        cols = pl.ds(pl.multiple_of(i * step, step), step)
        o = jnp.dot(attended, weight[:, cols], preferred_element_type=f32)
        video_out[:, cols] = o[:tok].astype(bf16)
        text_out[:, cols] = o[tok : tok + txt].astype(bf16)
        return 0

    lax.fori_loop(0, weight.shape[1] // step, project, 0)

    def finish(i, _):
        for kind in (KEY, VALUE):
            column_copy(kind, i).wait_send()
            forward(kind, i).wait_send()
        return 0

    lax.fori_loop(0, column - 1, finish, 0)
    for kind in (KEY, VALUE):
        forward(kind, column - 1).wait_send()
    for e in range(1, QUAD):
        for kind in (QUERY, FRESH_KEY, FRESH_VALUE):
            quad_copy(kind, e).wait_send()
        att_copy(e).wait_send()


def solution(mesh):
    n = mesh.shape["patch"]

    def body(*args):
        q_video, q_text, q_gain, weight = args[0], args[5], args[8], args[10]
        tok, width = q_video.shape
        txt, size = q_text.shape[0], q_gain.shape[0]
        pad = -(-(tok + txt) // 16) * 16
        part = width // QUAD
        heads = part // size
        column = n // 2
        quads = column // QUAD
        nblocks = 2 * quads + 1
        wide = QUAD * pad
        out = weight.shape[1]
        bf16, f32 = jnp.bfloat16, jnp.float32
        vmem = pl.BlockSpec(memory_space=pltpu.VMEM)
        dma = pltpu.SemaphoreType.DMA
        args = list(args)
        args[8], args[9] = args[8].reshape(1, size), args[9].reshape(1, size)
        return pl.pallas_call(
            functools.partial(kernel, n, tok, txt, size),
            out_shape=(
                jax.ShapeDtypeStruct((tok, out), bf16),
                jax.ShapeDtypeStruct((txt, out), bf16),
            ),
            in_specs=[vmem] * 10 + [pl.BlockSpec(memory_space=pl.ANY)],
            out_specs=(vmem, vmem),
            scratch_shapes=[
                pltpu.VMEM((pad, width), f32),
                pltpu.VMEM((5, QUAD, pad, part), bf16),
                pltpu.VMEM((2, 2, quads, QUAD, pad, part), bf16),
                pltpu.VMEM((3, QUAD, pad, part), bf16),
                pltpu.VMEM((3, wide, wide), f32),
                pltpu.VMEM((heads, wide, size), bf16),
                pltpu.VMEM((heads, wide, size), bf16),
                pltpu.VMEM((nblocks, heads, wide, wide), f32),
                pltpu.VMEM((heads, wide, size), f32),
                pltpu.VMEM((heads, wide, size), f32),
                pltpu.VMEM((QUAD, pad, part), bf16),
                pltpu.VMEM((QUAD, pad, part), bf16),
                pltpu.VMEM(weight.shape, bf16),
                dma((2, column)),
                dma((2, 2, column)),
                dma((2, column)),
                dma((3, QUAD)),
                dma((3, QUAD)),
                dma((QUAD,)),
                dma((QUAD,)),
                dma,
            ],
            compiler_params=pltpu.CompilerParams(
                collective_id=0, has_side_effects=True, vmem_limit_bytes=60 * 1024 * 1024
            ),
        )(*args)

    rows = P(("clips", "patch"), None)
    return jax.shard_map(
        body,
        mesh=mesh,
        in_specs=(rows,) * 8 + (P(),) * 3,
        out_specs=(rows, rows),
        check_vma=False,
    )
```

time: 134 us -> 48 us (0.36)
  Pallas kernels: 0 us -> 43.9 us
  blocking collectives: 42.2 us -> 0 us
  waiting for transfers between devices: 40.9 us -> 0 us
  between operations: 14.5 us -> 0.64 us
  local copies, waits for them, and re-layouts: 16.5 us -> 3.16 us
  matrix products: 13.2 us -> 0 us
  other arithmetic: 6.39 us -> 0 us
    pallas_call x0 -> x1, Pallas kernels: none -> 43.9 us  [body(): pl.pallas_call(functools.partial(kernel, n, tok, txt, size), out_shape=(j...]
    all_gather x2 -> x0, blocking collectives: 42.2 us -> none  [the longest x1 23.9 us: body(): lax.all_gather(text_keys, 'patch', axis=0, tiled=True)]
    all_gather x2 -> x0, waiting for transfers between devices: 40.2 us -> none  [the longest x1 37.7 us: body(): lax.all_gather(v_stale, 'patch', axis=0, tiled=True)]
    dot_general x5 -> x0, matrix products: 13.2 us -> none  [the longest x2 5.45 us: update(): jnp.einsum('hrp,phd->rhd', expo.astype(jnp.bfloat16), valued, preferred_e...]
    all_gather x2 -> x0, local copies, waits for them, and re-layouts: 8.72 us -> none  [the longest x1 4.36 us: body(): lax.all_gather(stale_keys, 'patch', axis=0, tiled=True)]
    reduce_sum x7 -> x0, other arithmetic: 2.46 us -> none  [the longest x2 1.61 us: update(): total = total * factor + jnp.sum(expo, axis=-1)]
    unnamed x42 -> x2, local copies, waits for them, and re-layouts: 5.38 us -> 3.16 us
    mul x5 -> x0, other arithmetic: 1.98 us -> none  [normed(): heads * heads]
  transfers between devices with their start and end apart: 2 -> 0, of which waited for: 2 -> 0; matrix products, arithmetic and copies ran while one was open for 9% -> 0% of each run, Pallas kernels for 0% -> 0%
where the time goes in v1:
time: 48 us; the launch traced here: 47.7 us
  Pallas kernels  43.9 us (91%)
  local copies, waits for them, and re-layouts  3.16 us (7%)
  between operations  0.64 us (1%)
    pallas_call x1, Pallas kernels, body(): pl.pallas_call(functools.partial(kernel, n, tok, txt, size), out_shape=(j...  43.9 us
    unnamed x2, local copies, waits for them, and re-layouts  3.16 us

profile of v1, /device:TPU:1, one launch (start us, length us, event | category | flops | bytes accessed | tf_op | source)
XLA Modules:
  0.0 47.7 jit_solution(14707552023383337795)
XLA Ops:
  0.6 43.9 %shard_map.122 = (bf16[72,3072]{1,0:T(8,128)(2,1)}, bf16[4,3072]{1,0:T(4,128)(2,1)}) custom-call(bf16[72,1536]{1,0:T(8,128)(2,1)} %q_video.1, bf16[72,1536]{1,0:T(8,128)(2,1)} %k_video.1, bf16[72,1536]{1,0:T(8,128)(2,1)} %v_video.1, bf16[72,1536]{1,0:T(8,128)(2,1)} %k_stale.1, bf16[72,1536]{1,0:T(8,128)(2,1)} %v_stale.1, bf16[4,1536]{1,0:T(4,128)(2,1)} %q_text.1, ...), custom_call_target="tpu_custom_call" | custom-call | tf_op jit(solution)/shard_map/pallas_call | solution.py:328
  44.5 1.8 %copy.15 = bf16[72,3072]{1,0:T(8,128)(2,1)} copy(bf16[72,3072]{1,0:T(8,128)(2,1)} %get-tuple-element.4) | data formatting | bytes 884736
  46.4 1.4 %copy.16 = bf16[4,3072]{1,0:T(4,128)(2,1)} copy(bf16[4,3072]{1,0:T(4,128)(2,1)} %get-tuple-element.5) | data formatting | bytes 49152

commit v2 on v1

--- a/solution.py
+++ b/solution.py
@@ -16,8 +16,8 @@
 def kernel(
     n, tok, txt, size,
     q_video, k_video, v_video, k_stale, v_stale, q_text, k_text, v_text, q_gain, k_gain, w_hbm,
-    video_out, text_out,
-    rows_f32, outgoing, kv, quad, bias, queries, keybuf, score, acc, total, att_out, att_in, weight,
+    out,
+    rows_f32, partial, outgoing, kv, quad, bias, queries, keybuf, score, acc, total, att_out, att_in, weight,
     send_sem, recv_sem, fwd_send, quad_send, quad_recv, att_send, att_recv, w_sem,
 ):
     f32, bf16 = jnp.float32, jnp.bfloat16
@@ -62,15 +62,22 @@
             lane = (h % heads) * size
             outgoing[kind, h // heads, :, lane : lane + size] = x.astype(bf16)
 
-    def distance(i):
-        return 1 + (i + column // 2 - 1) % (column - 1)
-
-    def column_copy(kind, i):
-        to = (spot + distance(i)) % column
+    planes = column // 2
+    partner_place = plane * 2 + 1 - core
+
+    def outward(i):
+        away = 1 + (i // 2 + planes // 2 - 1) % (planes - 1)
+        return ((plane + away) % planes) * 2 + (core + i) % 2
+
+    def inward(i):
+        away = 1 + (i // 2 + planes // 2 - 1) % (planes - 1)
+        return ((plane + planes - away) % planes) * 2 + (core + i) % 2
+
+    def column_copy(kind, to):
         return pltpu.make_async_remote_copy(
             src_ref=outgoing.at[kind, to % QUAD],
             dst_ref=kv.at[kind, 0, zz, mine],
-            send_sem=send_sem.at[kind, i],
+            send_sem=send_sem.at[kind, to],
             recv_sem=recv_sem.at[kind, 0, spot],
             device_id=device(to, side),
         )
@@ -96,12 +103,13 @@
 
     def send_column(kind):
         def go(i, _):
-            column_copy(kind, i).start()
+            column_copy(kind, outward(i)).start()
             return 0
 
+        column_copy(kind, partner_place).start()
         kv[kind, 0, zz, mine] = outgoing[kind, mine]
         forward(kind, spot).start()
-        lax.fori_loop(0, column - 1, go, 0)
+        lax.fori_loop(0, column - 2, go, 0)
 
     def quad_copy(kind, e):
         to = (mine + e) % QUAD
@@ -130,12 +138,14 @@
 
     def wait_and_forward(kind):
         def go(i, _):
-            place = (spot + column - distance(i)) % column
+            place = inward(i)
             column_arrival(kind, 0, place).wait_recv()
             forward(kind, place).start()
             return 0
 
-        lax.fori_loop(0, column - 1, go, 0)
+        column_arrival(kind, 0, partner_place).wait_recv()
+        forward(kind, partner_place).start()
+        lax.fori_loop(0, column - 2, go, 0)
 
     prepare(KEY, k_stale, k_text, k_gain)
     pl.semaphore_wait(barrier, column)
@@ -261,48 +271,60 @@
             device_id=device(zz * QUAD + to, side),
         )
 
-    def att_arrival(e):
-        slot = att_in.at[(mine + e) % QUAD]
-        return pltpu.make_async_remote_copy(
-            src_ref=slot,
-            dst_ref=slot,
-            send_sem=att_send.at[e],
-            recv_sem=att_recv.at[(mine + e) % QUAD],
-            device_id=across,
-        )
-
     for e in range(1, QUAD):
         att_copy(e).start()
     att_in[mine] = att_out[mine]
     w_copy.wait()
-    for e in range(1, QUAD):
-        att_arrival(e).wait_recv()
-
     step = 512
-    attended = jnp.concatenate([att_in[g] for g in range(QUAD)], axis=1)
-
-    def project(i, _):
-        cols = pl.ds(pl.multiple_of(i * step, step), step)
-        o = jnp.dot(attended, weight[:, cols], preferred_element_type=f32)
-        video_out[:, cols] = o[:tok].astype(bf16)
-        text_out[:, cols] = o[tok : tok + txt].astype(bf16)
-        return 0
-
-    lax.fori_loop(0, weight.shape[1] // step, project, 0)
+    half = mine // 2
+
+    def att_wait(place):
+        slot = att_in.at[place]
+        pltpu.make_async_remote_copy(
+            src_ref=slot, dst_ref=slot, send_sem=att_send.at[0], recv_sem=att_recv.at[place], device_id=across
+        ).wait_recv()
+
+    def project(which, last):
+        attended = jnp.concatenate([att_in[which * 2], att_in[which * 2 + 1]], axis=1)
+        depth = pl.ds(pl.multiple_of(which * 2 * part, 2 * part), 2 * part)
+
+        def go(i, _):
+            cols = pl.ds(pl.multiple_of(i * step, step), step)
+            o = jnp.dot(attended, weight[depth, cols], preferred_element_type=f32)
+            if last:
+                out[:, cols] = (partial[:, cols] + o).astype(bf16)
+            else:
+                partial[:, cols] = o
+            return 0
+
+        lax.fori_loop(0, weight.shape[1] // step, go, 0)
+
+    att_wait(half * 2 + 1 - core)
+    project(half, False)
+    for g in range(2):
+        att_wait((1 - half) * 2 + g)
+    project(1 - half, True)
 
     def finish(i, _):
         for kind in (KEY, VALUE):
-            column_copy(kind, i).wait_send()
-            forward(kind, i).wait_send()
-        return 0
-
-    lax.fori_loop(0, column - 1, finish, 0)
+            column_copy(kind, outward(i)).wait_send()
+            forward(kind, outward(i)).wait_send()
+        return 0
+
+    lax.fori_loop(0, column - 2, finish, 0)
     for kind in (KEY, VALUE):
-        forward(kind, column - 1).wait_send()
+        column_copy(kind, partner_place).wait_send()
+        forward(kind, partner_place).wait_send()
+        forward(kind, spot).wait_send()
     for e in range(1, QUAD):
         for kind in (QUERY, FRESH_KEY, FRESH_VALUE):
             quad_copy(kind, e).wait_send()
         att_copy(e).wait_send()
+
+
+def split(tok, both, video_out, text_out):
+    video_out[...] = both[:tok]
+    text_out[...] = both[tok : tok + text_out.shape[0]]
 
 
 def solution(mesh):
@@ -325,16 +347,14 @@
         dma = pltpu.SemaphoreType.DMA
         args = list(args)
         args[8], args[9] = args[8].reshape(1, size), args[9].reshape(1, size)
-        return pl.pallas_call(
+        both = pl.pallas_call(
             functools.partial(kernel, n, tok, txt, size),
-            out_shape=(
-                jax.ShapeDtypeStruct((tok, out), bf16),
-                jax.ShapeDtypeStruct((txt, out), bf16),
-            ),
+            out_shape=jax.ShapeDtypeStruct((pad, out), bf16),
             in_specs=[vmem] * 10 + [pl.BlockSpec(memory_space=pl.ANY)],
-            out_specs=(vmem, vmem),
+            out_specs=vmem,
             scratch_shapes=[
                 pltpu.VMEM((pad, width), f32),
+                pltpu.VMEM((pad, out), f32),
                 pltpu.VMEM((5, QUAD, pad, part), bf16),
                 pltpu.VMEM((2, 2, quads, QUAD, pad, part), bf16),
                 pltpu.VMEM((3, QUAD, pad, part), bf16),
@@ -360,6 +380,15 @@
                 collective_id=0, has_side_effects=True, vmem_limit_bytes=60 * 1024 * 1024
             ),
         )(*args)
+        return pl.pallas_call(
+            functools.partial(split, tok),
+            out_shape=(
+                jax.ShapeDtypeStruct((tok, out), bf16),
+                jax.ShapeDtypeStruct((txt, out), bf16),
+            ),
+            in_specs=[vmem],
+            out_specs=(vmem, vmem),
+        )(both)
 
     rows = P(("clips", "patch"), None)
     return jax.shard_map(

time: 48 us -> 45.8 us (0.954)
  local copies, waits for them, and re-layouts: 3.16 us -> 0 us
  Pallas kernels: 43.9 us -> 45 us
    unnamed x2 -> x0, local copies, waits for them, and re-layouts: 3.16 us -> none
    pallas_call x1 -> x2, Pallas kernels: 43.9 us -> 45 us  [the longest x1 43.1 us: body(): pl.pallas_call(functools.partial(kernel, n, tok, txt, size), out_shape=ja...]
where the time goes in v2:
time: 45.8 us; the launch traced here: 45.6 us
  Pallas kernels  45 us (98%)
  between operations  0.64 us (1%)
    pallas_call x1, Pallas kernels, body(): pl.pallas_call(functools.partial(kernel, n, tok, txt, size), out_shape=ja...  43.1 us
    pallas_call x1, Pallas kernels, body(): pl.pallas_call(functools.partial(split, tok), out_shape=(jax.ShapeDtypeSt...  1.82 us

profile of v2, /device:TPU:1, one launch (start us, length us, event | category | flops | bytes accessed | tf_op | source)
XLA Modules:
  0.0 45.6 jit_solution(12090391425314227325)
XLA Ops:
  0.6 43.1 %shard_map.122.both = bf16[80,3072]{1,0:T(8,128)(2,1)} custom-call(bf16[72,1536]{1,0:T(8,128)(2,1)} %q_video.1, bf16[72,1536]{1,0:T(8,128)(2,1)} %k_video.1, bf16[72,1536]{1,0:T(8,128)(2,1)} %v_video.1, bf16[72,1536]{1,0:T(8,128)(2,1)} %k_stale.1, bf16[72,1536]{1,0:T(8,128)(2,1)} %v_stale.1, bf16[4,1536]{1,0:T(4,128)(2,1)} %q_text.1, ...), custom_call_target="tpu_custom_call" | custom-call | tf_op jit(solution)/shard_map/pallas_call | solution.py:350
  43.8 1.8 %shard_map.123 = (bf16[72,3072]{1,0:T(8,128)(2,1)}, bf16[4,3072]{1,0:T(4,128)(2,1)}) custom-call(bf16[80,3072]{1,0:T(8,128)(2,1)} %shard_map.122.both), custom_call_target="tpu_custom_call" | custom-call | tf_op jit(solution)/shard_map/pallas_call | solution.py:383

commit v3 on v2

--- a/solution.py
+++ b/solution.py
@@ -238,15 +238,16 @@
             o = jnp.dot(score[b, h].astype(bf16), values(lane), preferred_element_type=f32)
             acc[h] = o if first else acc[h] + o
 
+    value_block(1, gathered(VALUE, 0, zz), True)
+
+    def own_values(e, _):
+        value_block(1 + e, gathered(VALUE, 0, (zz + e) % quads))
+        return 0
+
+    lax.fori_loop(1, quads, own_values, 0)
     for e in range(1, QUAD):
         quad_arrival(FRESH_VALUE, e).wait_recv()
-    value_block(0, exchanged(FRESH_VALUE), True)
-
-    def own_values(e, _):
-        value_block(1 + e, gathered(VALUE, 0, (zz + e) % quads))
-        return 0
-
-    lax.fori_loop(0, quads, own_values, 0)
+    value_block(0, exchanged(FRESH_VALUE))
 
     def other_values(e, _):
         z = (zz + e) % quads

time: 45.8 us -> 45.7 us (level)
  no operation moved by 1% of the time
where the time goes in v3:
time: 45.7 us; the launch traced here: 45.5 us
  Pallas kernels  44.8 us (98%)
  between operations  0.64 us (1%)
    pallas_call x1, Pallas kernels, body(): pl.pallas_call(functools.partial(kernel, n, tok, txt, size), out_shape=ja...  43 us
    pallas_call x1, Pallas kernels, body(): pl.pallas_call(functools.partial(split, tok), out_shape=(jax.ShapeDtypeSt...  1.82 us

profile of v3, /device:TPU:1, one launch (start us, length us, event | category | flops | bytes accessed | tf_op | source)
XLA Modules:
  0.0 45.5 jit_solution(11751380223900723752)
XLA Ops:
  0.6 43.0 %shard_map.122.both = bf16[80,3072]{1,0:T(8,128)(2,1)} custom-call(bf16[72,1536]{1,0:T(8,128)(2,1)} %q_video.1, bf16[72,1536]{1,0:T(8,128)(2,1)} %k_video.1, bf16[72,1536]{1,0:T(8,128)(2,1)} %v_video.1, bf16[72,1536]{1,0:T(8,128)(2,1)} %k_stale.1, bf16[72,1536]{1,0:T(8,128)(2,1)} %v_stale.1, bf16[4,1536]{1,0:T(4,128)(2,1)} %q_text.1, ...), custom_call_target="tpu_custom_call" | custom-call | tf_op jit(solution)/shard_map/pallas_call | solution.py:351
  43.6 1.8 %shard_map.123 = (bf16[72,3072]{1,0:T(8,128)(2,1)}, bf16[4,3072]{1,0:T(4,128)(2,1)}) custom-call(bf16[80,3072]{1,0:T(8,128)(2,1)} %shard_map.122.both), custom_call_target="tpu_custom_call" | custom-call | tf_op jit(solution)/shard_map/pallas_call | solution.py:384
